TPU v7x, 128 devices: a whole 4x4x4 slice. The times are simulated.
128 devices in a mesh: pgrp: 4 (over y_lo, core), srow: 32 (over x, z, y_hi).
Axes of the slice: x: 4, y: 4 (y_hi: 2, y_lo: 2; y = y_hi * 2 + y_lo), z: 4, core: 2. Of those that a mesh axis runs over, the one named last changes fastest.
Arguments:
- kernel: bfloat16 [608, 224, 512], P('srow', None, 'pgrp'), may hold values from -0.0234375 to 0.0234375
- probes: bfloat16 [4, 608, 224], P(None, 'srow', 'pgrp'), may hold values from -6 to 6
- prior_var: float32 [512], P('pgrp'), may hold values from 0.3 to 3
- noise_var: float32 [608], P('srow'), may hold values from 0.1 to 1
Outputs:
- hessian_probes: float32 [4, 608, 224], P(None, 'srow', 'pgrp')
All inputs are finite; a program needn't handle non-finite values.
Results may differ from a plain program's by a relative error of at most 0.0022.
Values may be sent and summed in bfloat16 or wider, within the bound.
A program may use at most 64 MiB of HBM per device.

v0:
```python
import math

import jax
import jax.numpy as jnp
from jax import lax
from jax.sharding import PartitionSpec as P


def in_blocks(shard, dim, length):
    before, after = (shard.shape[:dim], shard.shape[dim + 1 :])
    return jnp.moveaxis(shard.reshape(*before, length, -1, *after), dim, 0)


def sum_at_owner(shard, axis, dim):
    length = lax.axis_size(axis)
    pieces = lax.all_to_all(in_blocks(shard, dim, length), axis, 0, 0, tiled=True)
    return jnp.sum(pieces, axis=0)


def laid_out(pieces, dim):
    pieces = jnp.moveaxis(pieces, 0, dim)
    shape = pieces.shape
    return pieces.reshape(*shape[:dim], shape[dim] * shape[dim + 1], *shape[dim + 2 :])


def from_everyone(shard, axis):
    length = lax.axis_size(axis)
    return lax.all_to_all(
        jnp.broadcast_to(shard[None], (length, *shard.shape)), axis, 0, 0, tiled=True
    )


def gather_directly(shard, axis, dim):
    return laid_out(from_everyone(shard, axis), dim)


def lag_block(length):
    return math.gcd(length, 28)


def correlate(series, kernel):
    length = series.shape[2]
    width = lag_block(length)
    padded = jnp.concatenate([series, jnp.zeros_like(series)], axis=2)
    offsets = jnp.arange(width, dtype=jnp.int32)

    def correlate_one_turn(turn, total):
        first = (turn * width).astype(jnp.int32)

        def correlate_shifted(offset):
            return lax.dynamic_slice_in_dim(padded, first + offset, length, 2)

        window = jax.vmap(correlate_shifted, out_axes=2)(offsets)
        kernel_part = lax.dynamic_slice_in_dim(kernel, first, width, 1)
        return total + jnp.einsum(
            "sjp,nsjt->npt", kernel_part, window, preferred_element_type=jnp.float32
        )

    start = jnp.zeros((series.shape[0], kernel.shape[2], length), jnp.float32)
    return lax.fori_loop(0, length // width, correlate_one_turn, start)


def convolve(params, kernel):
    length = params.shape[2]
    width = lag_block(length)
    padded = jnp.concatenate([jnp.zeros_like(params), params], axis=2)
    offsets = jnp.arange(width, dtype=jnp.int32)

    def convolve_one_turn(turn, total):
        first = (turn * width).astype(jnp.int32)

        def convolve_shifted(offset):
            return lax.dynamic_slice_in_dim(padded, length - first - offset, length, 2)

        window = jax.vmap(convolve_shifted, out_axes=2)(offsets)
        kernel_part = lax.dynamic_slice_in_dim(kernel, first, width, 1)
        return total + jnp.einsum(
            "sjp,npjt->nst", kernel_part, window, preferred_element_type=jnp.float32
        )

    start = jnp.zeros((params.shape[0], kernel.shape[0], length), jnp.float32)
    return lax.fori_loop(0, length // width, convolve_one_turn, start)


def on_device(kernel, probes, prior_var, noise_var):
    series = lax.all_gather(probes, "pgrp", axis=2, tiled=True)
    adjoint = correlate(series, kernel)
    shares = sum_at_owner(adjoint, "srow", 1)
    per_dev = shares.shape[1]
    local_prior = lax.dynamic_slice_in_dim(prior_var, lax.axis_index("srow") * per_dev, per_dev)
    scaled = (shares * local_prior[None, :, None]).astype(jnp.bfloat16)
    params = gather_directly(scaled, "srow", 1)
    forward = convolve(params, kernel)
    summed = sum_at_owner(forward, "pgrp", 2)
    return summed + noise_var[None, :, None] * probes.astype(jnp.float32)


def solution(mesh):
    placed = (P("srow", None, "pgrp"), P(None, "srow", "pgrp"), P("pgrp"), P("srow"))
    return jax.shard_map(
        on_device, mesh=mesh, in_specs=placed, out_specs=P(None, "srow", "pgrp"), check_vma=False
    )
```

profile of v0, /device:TPU:1, one launch (start us, length us, event | category | flops | bytes accessed | tf_op | source)
XLA Modules:
  0.0 323.9 jit_solution(5302327209381321763)
XLA Ops:
  8.0 150.1 %while.28 = (s32[]{:T(128)}, f32[4,128,224]{1,2,0:T(8,128)S(1)}, bf16[4,19,448]{1,0,2:T(4,128)(2,1)S(1)}, bf16[19,224,128]{2,1,0:T(8,128)(2,1)}, s32[]{:T(128)}, /*index=5*/s32[]{:T(128)}, s32[]{:T(128)}, s32[]{:T(128)}) while((s32[]{:T(128)}, f32[4,128,224]{1,2,0:T(8,128)S(1)}, bf16[4,19,448]{1,0,2:T(4,128)(2,1)S(1)}, ...), condition=%wide.region_1.0_spmd.clone, body=%wide.region_0.0_spmd.clone.sunk | while | flops 122257584 | bytes 5840469 | solution.py:60
  8.1 8.8 %gather_fusion = bf16[28,4,19,224]{2,1,3,0:T(4,128)(2,1)} fusion(bf16[4,19,448]{1,0,2:T(4,128)(2,1)S(1)} %get-tuple-element.325, s32[28]{0:T(128)S(1)} %fusion.32), kind=kCustom, calls=%fused_computation.clone.clone.1 | custom fusion | bytes 1907024 | tf_op jit(solution)/shard_map/while/body/eval_jaxpr/vmap()/gather | solution.py:51
  16.9 8.3 %copy.41 = bf16[4,19,28,224]{3,2,1,0:T(8,128)(2,1)S(1)} copy(bf16[4,19,28,224]{1,0,3,2:T(4,128)(2,1)} %bitcast.67) | data formatting | bytes 1906688 | tf_op jit(solution)/shard_map/while/body/eval_jaxpr/vmap()/transpose | solution.py:53
  26.8 8.8 %gather_fusion = bf16[28,4,19,224]{2,1,3,0:T(4,128)(2,1)} fusion(bf16[4,19,448]{1,0,2:T(4,128)(2,1)S(1)} %get-tuple-element.325, s32[28]{0:T(128)S(1)} %fusion.32), kind=kCustom, calls=%fused_computation.clone.clone.1 | custom fusion | bytes 1907024 | tf_op jit(solution)/shard_map/while/body/eval_jaxpr/vmap()/gather | solution.py:51
  35.7 8.3 %copy.41 = bf16[4,19,28,224]{3,2,1,0:T(8,128)(2,1)S(1)} copy(bf16[4,19,28,224]{1,0,3,2:T(4,128)(2,1)} %bitcast.67) | data formatting | bytes 1906688 | tf_op jit(solution)/shard_map/while/body/eval_jaxpr/vmap()/transpose | solution.py:53
  45.6 8.8 %gather_fusion = bf16[28,4,19,224]{2,1,3,0:T(4,128)(2,1)} fusion(bf16[4,19,448]{1,0,2:T(4,128)(2,1)S(1)} %get-tuple-element.325, s32[28]{0:T(128)S(1)} %fusion.32), kind=kCustom, calls=%fused_computation.clone.clone.1 | custom fusion | bytes 1907024 | tf_op jit(solution)/shard_map/while/body/eval_jaxpr/vmap()/gather | solution.py:51
  64.4 8.8 %gather_fusion = bf16[28,4,19,224]{2,1,3,0:T(4,128)(2,1)} fusion(bf16[4,19,448]{1,0,2:T(4,128)(2,1)S(1)} %get-tuple-element.325, s32[28]{0:T(128)S(1)} %fusion.32), kind=kCustom, calls=%fused_computation.clone.clone.1 | custom fusion | bytes 1907024 | tf_op jit(solution)/shard_map/while/body/eval_jaxpr/vmap()/gather | solution.py:51
  83.1 8.8 %gather_fusion = bf16[28,4,19,224]{2,1,3,0:T(4,128)(2,1)} fusion(bf16[4,19,448]{1,0,2:T(4,128)(2,1)S(1)} %get-tuple-element.325, s32[28]{0:T(128)S(1)} %fusion.32), kind=kCustom, calls=%fused_computation.clone.clone.1 | custom fusion | bytes 1907024 | tf_op jit(solution)/shard_map/while/body/eval_jaxpr/vmap()/gather | solution.py:51
  101.9 8.8 %gather_fusion = bf16[28,4,19,224]{2,1,3,0:T(4,128)(2,1)} fusion(bf16[4,19,448]{1,0,2:T(4,128)(2,1)S(1)} %get-tuple-element.325, s32[28]{0:T(128)S(1)} %fusion.32), kind=kCustom, calls=%fused_computation.clone.clone.1 | custom fusion | bytes 1907024 | tf_op jit(solution)/shard_map/while/body/eval_jaxpr/vmap()/gather | solution.py:51
  120.7 8.8 %gather_fusion = bf16[28,4,19,224]{2,1,3,0:T(4,128)(2,1)} fusion(bf16[4,19,448]{1,0,2:T(4,128)(2,1)S(1)} %get-tuple-element.325, s32[28]{0:T(128)S(1)} %fusion.32), kind=kCustom, calls=%fused_computation.clone.clone.1 | custom fusion | bytes 1907024 | tf_op jit(solution)/shard_map/while/body/eval_jaxpr/vmap()/gather | solution.py:51
  139.4 8.8 %gather_fusion = bf16[28,4,19,224]{2,1,3,0:T(4,128)(2,1)} fusion(bf16[4,19,448]{1,0,2:T(4,128)(2,1)S(1)} %get-tuple-element.325, s32[28]{0:T(128)S(1)} %fusion.32), kind=kCustom, calls=%fused_computation.clone.clone.1 | custom fusion | bytes 1907024 | tf_op jit(solution)/shard_map/while/body/eval_jaxpr/vmap()/gather | solution.py:51
  148.3 8.3 %copy.41 = bf16[4,19,28,224]{3,2,1,0:T(8,128)(2,1)S(1)} copy(bf16[4,19,28,224]{1,0,3,2:T(4,128)(2,1)} %bitcast.67) | data formatting | bytes 1906688 | tf_op jit(solution)/shard_map/while/body/eval_jaxpr/vmap()/transpose | solution.py:53
  159.2 10.6 %all-to-all-start = ((f32[32,4,4,224]{3,1,2,0:T(4,128)}), f32[32,4,4,224]{3,1,2,0:T(4,128)S(1)}, u32[]{:S(2)}, u32[]{:S(2)}) async-start(f32[32,4,4,224]{3,1,2,0:T(4,128)} %bitcast.1), calls=%async_computation | async-start | bytes 1048576 | tf_op jit(solution)/shard_map/all_to_all | solution.py:16
  169.8 12.7 %all-to-all-done = f32[32,4,4,224]{3,1,2,0:T(4,128)S(1)} async-done(((f32[32,4,4,224]{3,1,2,0:T(4,128)}), f32[32,4,4,224]{3,1,2,0:T(4,128)S(1)}, u32[]{:S(2)}, u32[]{:S(2)}) %all-to-all-start) | async-done | bytes 458784 | tf_op jit(solution)/shard_map/all_to_all | solution.py:16
  187.5 9.5 %all-to-all-done.1 = bf16[32,4,4,224]{3,1,2,0:T(4,128)(2,1)S(1)} async-done(((bf16[32,4,4,224]{3,1,2,0:T(4,128)(2,1)}), bf16[32,4,4,224]{3,1,2,0:T(4,128)(2,1)S(1)}, u32[]{:S(2)}, u32[]{:S(2)}) %all-to-all-start.1) | async-done | bytes 229408 | tf_op jit(solution)/shard_map/all_to_all | solution.py:28
  197.5 115.4 %while.29 = (s32[]{:T(128)}, f32[4,19,224]{2,1,0:T(8,128)S(1)}, bf16[4,128,448]{1,0,2:T(4,128)(2,1)S(1)}, bf16[19,224,128]{2,1,0:T(8,128)(2,1)}, s32[]{:T(128)}, /*index=5*/s32[]{:T(128)}, s32[]{:T(128)}, s32[]{:T(128)}) while((s32[]{:T(128)}, f32[4,19,224]{2,1,0:T(8,128)S(1)}, bf16[4,128,448]{1,0,2:T(4,128)(2,1)S(1)}, ...), condition=%wide.region_4.0_spmd.clone, body=%wide.region_3.0_spmd.clone.sunk | while | flops 122062256 | bytes 19812960 | solution.py:82
  198.5 8.8 %gather_fusion.1 = bf16[28,4,128,224]{2,1,3,0:T(4,128)(2,1)} fusion(bf16[4,128,448]{1,0,2:T(4,128)(2,1)S(1)} %get-tuple-element.349, s32[28]{0:T(128)S(1)} %fusion.35), kind=kCustom, calls=%fused_computation.1.clone.clone.1 | custom fusion | bytes 12845392 | tf_op jit(solution)/shard_map/while/body/eval_jaxpr/vmap()/gather | solution.py:73
  212.9 8.8 %gather_fusion.1 = bf16[28,4,128,224]{2,1,3,0:T(4,128)(2,1)} fusion(bf16[4,128,448]{1,0,2:T(4,128)(2,1)S(1)} %get-tuple-element.349, s32[28]{0:T(128)S(1)} %fusion.35), kind=kCustom, calls=%fused_computation.1.clone.clone.1 | custom fusion | bytes 12845392 | tf_op jit(solution)/shard_map/while/body/eval_jaxpr/vmap()/gather | solution.py:73
  227.3 8.8 %gather_fusion.1 = bf16[28,4,128,224]{2,1,3,0:T(4,128)(2,1)} fusion(bf16[4,128,448]{1,0,2:T(4,128)(2,1)S(1)} %get-tuple-element.349, s32[28]{0:T(128)S(1)} %fusion.35), kind=kCustom, calls=%fused_computation.1.clone.clone.1 | custom fusion | bytes 12845392 | tf_op jit(solution)/shard_map/while/body/eval_jaxpr/vmap()/gather | solution.py:73
  241.8 8.8 %gather_fusion.1 = bf16[28,4,128,224]{2,1,3,0:T(4,128)(2,1)} fusion(bf16[4,128,448]{1,0,2:T(4,128)(2,1)S(1)} %get-tuple-element.349, s32[28]{0:T(128)S(1)} %fusion.35), kind=kCustom, calls=%fused_computation.1.clone.clone.1 | custom fusion | bytes 12845392 | tf_op jit(solution)/shard_map/while/body/eval_jaxpr/vmap()/gather | solution.py:73
  256.2 8.8 %gather_fusion.1 = bf16[28,4,128,224]{2,1,3,0:T(4,128)(2,1)} fusion(bf16[4,128,448]{1,0,2:T(4,128)(2,1)S(1)} %get-tuple-element.349, s32[28]{0:T(128)S(1)} %fusion.35), kind=kCustom, calls=%fused_computation.1.clone.clone.1 | custom fusion | bytes 12845392 | tf_op jit(solution)/shard_map/while/body/eval_jaxpr/vmap()/gather | solution.py:73
  270.6 8.8 %gather_fusion.1 = bf16[28,4,128,224]{2,1,3,0:T(4,128)(2,1)} fusion(bf16[4,128,448]{1,0,2:T(4,128)(2,1)S(1)} %get-tuple-element.349, s32[28]{0:T(128)S(1)} %fusion.35), kind=kCustom, calls=%fused_computation.1.clone.clone.1 | custom fusion | bytes 12845392 | tf_op jit(solution)/shard_map/while/body/eval_jaxpr/vmap()/gather | solution.py:73
  285.0 8.8 %gather_fusion.1 = bf16[28,4,128,224]{2,1,3,0:T(4,128)(2,1)} fusion(bf16[4,128,448]{1,0,2:T(4,128)(2,1)S(1)} %get-tuple-element.349, s32[28]{0:T(128)S(1)} %fusion.35), kind=kCustom, calls=%fused_computation.1.clone.clone.1 | custom fusion | bytes 12845392 | tf_op jit(solution)/shard_map/while/body/eval_jaxpr/vmap()/gather | solution.py:73
  299.4 8.8 %gather_fusion.1 = bf16[28,4,128,224]{2,1,3,0:T(4,128)(2,1)} fusion(bf16[4,128,448]{1,0,2:T(4,128)(2,1)S(1)} %get-tuple-element.349, s32[28]{0:T(128)S(1)} %fusion.35), kind=kCustom, calls=%fused_computation.1.clone.clone.1 | custom fusion | bytes 12845392 | tf_op jit(solution)/shard_map/while/body/eval_jaxpr/vmap()/gather | solution.py:73
  (74 shorter events, 124.4 us)
Async XLA Ops:
  8.0 161.7 %copy-start.2 = (f32[128]{0:T(128)S(1)}, f32[128]{0:T(128)}, u32[]{:S(2)}) copy-start(f32[128]{0:T(128)} %param.10) | copy-start | bytes 1540
  159.2 23.4 %all-to-all-start = ((f32[32,4,4,224]{3,1,2,0:T(4,128)}), f32[32,4,4,224]{3,1,2,0:T(4,128)S(1)}, u32[]{:S(2)}, u32[]{:S(2)}) async-start(f32[32,4,4,224]{3,1,2,0:T(4,128)} %bitcast.1), calls=%async_computation | async-start | bytes 1048576 | tf_op jit(solution)/shard_map/all_to_all | solution.py:16
  183.5 13.6 %all-to-all-start.1 = ((bf16[32,4,4,224]{3,1,2,0:T(4,128)(2,1)}), bf16[32,4,4,224]{3,1,2,0:T(4,128)(2,1)S(1)}, u32[]{:S(2)}, u32[]{:S(2)}) async-start(bf16[32,4,4,224]{3,1,2,0:T(4,128)(2,1)} %broadcast_in_dim.24), calls=%async_computation.1 | async-start | bytes 524288 | tf_op jit(solution)/shard_map/all_to_all | solution.py:28
  197.4 125.8 %copy-start = (bf16[4,19,56]{2,0,1:T(4,128)(2,1)S(1)}, bf16[4,19,56]{2,0,1:T(4,128)(2,1)}, u32[]{:S(2)}) copy-start(bf16[4,19,56]{2,0,1:T(4,128)(2,1)} %param.9) | copy-start | bytes 25540
  197.4 125.8 %copy-start.1 = (f32[19]{0:T(128)S(1)}, f32[19]{0:T(128)}, u32[]{:S(2)}) copy-start(f32[19]{0:T(128)} %param.11) | copy-start | bytes 232
where the time goes:
time: 326 us; the launch traced here: 324 us
  local copies, waits for them, and re-layouts  220 us (67%)
  matrix products  49.2 us (15%)
  waiting for transfers between devices  22.2 us (7%)
  blocking collectives  15.3 us (5%)
  starting transfers between devices  14.6 us (4%)
    gather x8, local copies, waits for them, and re-layouts, correlate_shifted(): return lax.dynamic_slice_in_dim(padded, first + offset, length, 2)  70.5 us
    gather x8, local copies, waits for them, and re-layouts, convolve_shifted(): return lax.dynamic_slice_in_dim(padded, length - first - offset, length, 2)  70.5 us
    transpose x8, local copies, waits for them, and re-layouts, correlate_one_turn(): window = jax.vmap(correlate_shifted, out_axes=2)(offsets)  66.7 us
    dot_general x8, matrix products, convolve_one_turn(): jnp.einsum('sjp,npjt->nst', kernel_part, window, preferred_element_type=j...  36.7 us
    all_to_all x1, waiting for transfers between devices, sum_at_owner(): lax.all_to_all(in_blocks(shard, dim, length), axis, 0, 0, tiled=True)  12.7 us
    dot_general x8, matrix products, correlate_one_turn(): jnp.einsum('sjp,nsjt->npt', kernel_part, window, preferred_element_type=j...  12.5 us
    all_to_all x1, starting transfers between devices, sum_at_owner(): lax.all_to_all(in_blocks(shard, dim, length), axis, 0, 0, tiled=True)  10.6 us
    all_to_all x1, waiting for transfers between devices, from_everyone(): lax.all_to_all(jnp.broadcast_to(shard[None], (length, *shard.shape)), axi...  9.5 us
  transfers between devices with their start and end apart: 2, of which 2 were waited for; matrix products, arithmetic and copies ran while one was open for 0% of the time, Pallas kernels for 0%

commit v1 on v0

v1 whole, which is shorter than its diff:
```python
import functools

import jax
import jax.numpy as jnp
from jax import lax
from jax.experimental import pallas as pl
from jax.experimental.pallas import tpu as pltpu
from jax.sharding import PartitionSpec as P

MESH = pl.DeviceIdType.MESH
F32 = jnp.float32
BF16 = jnp.bfloat16

NV, NS, NT, NP = 4, 19, 224, 128
NQ, NR = 4, 32
STEP = 32
NH = NT // STEP
PAIRS = (NH + 1) // 2
ROWS = NV * STEP
WIDE = 256
LEAD = NT - STEP
TALL = LEAD + WIDE
PART = NT // NQ
HALF = 64
SROWS = 24
PROWS = 2 * SROWS


def owner_of(h, n):
    return 8 * n + 2 * ((n + h // 2) % 4) + h % 2


def block_of(r):
    n = r // 8
    h = 2 * lax.rem(lax.rem(r // 2, 4) - n + 4, 4) + lax.rem(r, 2)
    return h, n


def kernel_body(
    probes_ref, prior_ref, noise_ref, k_hbm, out_ref,
    kpad, base, y_ref, pf, psend, precv, rsend, rrecv, xall, f_ref, fsend, frecv,
    k_sem, ps_sem, pr_sem, rs_sem, rr_sem, xs_sem, xr_sem, fs_sem, fr_sem,
):
    me = lax.axis_index("srow")
    grp = lax.axis_index("pgrp")
    my_h, my_n = block_of(me)
    mine = my_h * NV + my_n
    owns = my_h < NH

    barrier = pltpu.get_barrier_semaphore()

    def greet(d, _):
        pl.semaphore_signal(
            barrier, inc=1, device_id={"srow": lax.rem(me + d, NR)}, device_id_type=MESH
        )
        return 0

    for d in range(1, NQ):
        pl.semaphore_signal(
            barrier, inc=1, device_id={"pgrp": lax.rem(grp + d, NQ)}, device_id_type=MESH
        )
    lax.fori_loop(1, NR, greet, 0)

    k_copy = pltpu.make_async_copy(k_hbm, kpad.at[:, pl.ds(LEAD, NT), :], k_sem)
    k_copy.start()

    pf[...] = jnp.zeros_like(pf)
    for n in range(NV):
        row, lane = (n % 2) * SROWS, (n // 2) * HALF
        pf[row : row + NS, lane : lane + PART] = probes_ref[n].astype(F32)
    psend[...] = pf[...].astype(BF16)
    kpad[:, 0:LEAD, :] = jnp.zeros((NS, LEAD, NP), BF16)
    kpad[:, LEAD + NT : TALL, :] = jnp.zeros((NS, TALL - LEAD - NT, NP), BF16)
    f_ref[...] = jnp.zeros_like(f_ref)

    pl.semaphore_wait(barrier, NQ - 1 + NR - 1)

    def probe_copy(d):
        to = lax.rem(grp + d, NQ)
        return pltpu.make_async_remote_copy(
            src_ref=psend, dst_ref=precv.at[d - 1], send_sem=ps_sem.at[d - 1],
            recv_sem=pr_sem.at[d - 1], device_id={"pgrp": to}, device_id_type=MESH,
        )

    for d in range(1, NQ):
        probe_copy(d).start()
    lanes = lax.broadcasted_iota(jnp.int32, (SROWS, NP), 1)
    zeros = jnp.zeros((SROWS, WIDE - NP), F32)

    def place(part, group):
        for n in range(NV):
            row, lane = (n % 2) * SROWS, (n // 2) * HALF
            inside = (lanes >= lane) & (lanes < lane + PART)
            piece = jnp.where(inside, part[row : row + SROWS, :].astype(F32), 0.0)
            wide = jnp.concatenate([piece, zeros], axis=1)
            shift = lax.rem(group * PART + (WIDE - (STEP - 1) - lane), WIDE)
            y_ref[n] += pltpu.roll(wide, shift, 1)

    y_ref[...] = jnp.zeros_like(y_ref)
    place(psend, grp)
    for d in range(1, NQ):
        probe_copy(d).wait_recv()
        place(precv[d - 1], lax.rem(grp + NQ - d, NQ))

    inside_wide = lax.broadcasted_iota(jnp.int32, (STEP, WIDE), 1) < NT

    def make_base(s, _):
        for n in range(NV):
            line = jnp.broadcast_to(y_ref[n, pl.ds(s, 1), :], (STEP, WIDE))
            turned = pltpu.roll(line, 0, 1, stride=1, stride_axis=0)
            turned = jnp.where(inside_wide, turned, 0.0)
            base[s, n * STEP : (n + 1) * STEP, :] = turned.astype(BF16)
        return 0

    lax.fori_loop(0, NS, make_base, 0)
    k_copy.wait()

    def share_copy(h, n, slot):
        return pltpu.make_async_remote_copy(
            src_ref=rsend.at[h * NV + n], dst_ref=rrecv.at[slot], send_sem=rs_sem.at[h * NV + n],
            recv_sem=rr_sem.at[slot], device_id={"srow": owner_of(h, n)}, device_id_type=MESH,
        )

    def spans(hp):
        return [h for h in (2 * hp, 2 * hp + 1) if h < NH]

    for hp in range(PAIRS):
        hs = spans(hp)

        def add_sensor(s, acc):
            w = jnp.concatenate(
                [kpad[s, LEAD - STEP * h : LEAD - STEP * h + WIDE, :] for h in hs], axis=1
            )
            return acc + jnp.dot(base[s], w, preferred_element_type=F32)

        acc = lax.fori_loop(0, NS, add_sensor, jnp.zeros((ROWS, NP * len(hs)), F32))
        for j, h in enumerate(hs):
            for n in range(NV):
                rsend[h * NV + n] = acc[n * STEP : (n + 1) * STEP, j * NP : (j + 1) * NP]

        def send_share(j, _):
            j = lax.rem(j + me, NV * len(hs))
            n, h = lax.rem(j, NV), hs[0] + j // NV

            @pl.when(owner_of(h, n) != me)
            def _():
                share_copy(h, n, me).start()

            return 0

        lax.fori_loop(0, NV * len(hs), send_share, 0)

    def param_copy(d):
        to = lax.rem(me + d, NR)
        return pltpu.make_async_remote_copy(
            src_ref=xall.at[mine], dst_ref=xall.at[mine], send_sem=xs_sem.at[d],
            recv_sem=xr_sem.at[mine], device_id={"srow": to}, device_id_type=MESH,
        )

    @pl.when(owns)
    def _():
        def take(d, total):
            slot = lax.rem(me + d, NR)
            share_copy(my_h, my_n, slot).wait_recv()
            return total + rrecv[slot]

        total = lax.fori_loop(1, NR, take, rsend[mine])
        scaled = total * prior_ref[...]
        row = lax.broadcasted_iota(jnp.int32, (STEP, STEP), 0)
        col = lax.broadcasted_iota(jnp.int32, (STEP, STEP), 1)
        flip = (row + col == STEP - 1).astype(BF16)
        xall[mine] = jnp.dot(flip, scaled.astype(BF16), preferred_element_type=F32).astype(BF16)

        def send_params(d, _):
            param_copy(d).start()
            return 0

        lax.fori_loop(1, NR, send_params, 0)

    def wait_block(b, _):
        @pl.when(b != mine)
        def _():
            pltpu.make_async_remote_copy(
                src_ref=xall.at[b], dst_ref=xall.at[b], send_sem=xs_sem.at[0],
                recv_sem=xr_sem.at[b], device_id={"srow": me}, device_id_type=MESH,
            ).wait_recv()

        return 0

    lax.fori_loop(0, NH * NV, wait_block, 0)

    def x_of(h):
        return xall[h * NV : (h + 1) * NV].reshape(ROWS, NP)

    inside_rows = lax.broadcasted_iota(jnp.int32, (ROWS, WIDE), 1) < NT

    def forward_sensor(s, _):
        z = jnp.zeros((ROWS, WIDE), F32)
        for hp in range(PAIRS):
            hs = spans(hp)
            x = jnp.concatenate([x_of(h) for h in hs], axis=1)
            w = jnp.concatenate(
                [kpad[s, LEAD - STEP * h : LEAD - STEP * h + WIDE, :] for h in hs], axis=1
            )
            z = z + lax.dot_general(x, w, (((1,), (1,)), ((), ())), preferred_element_type=F32)
        z = jnp.where(inside_rows, z, 0.0)
        for n in range(NV):
            turned = pltpu.roll(z[n * STEP : (n + 1) * STEP, :], 0, 1, stride=1, stride_axis=0)
            f_ref[n, pl.ds(s, 1), :] = jnp.sum(turned, axis=0, keepdims=True)
        return 0

    lax.fori_loop(0, NS, forward_sensor, 0)

    first = lanes < HALF
    for q in range(NQ):
        for n in range(2):
            low = pltpu.roll(f_ref[n], (WIDE - PART * q) % WIDE, 1)[:, :NP]
            high = pltpu.roll(f_ref[n + 2], (WIDE - PART * q + HALF) % WIDE, 1)[:, :NP]
            fsend[q, n * SROWS : (n + 1) * SROWS, :] = jnp.where(first, low, high)

    def sum_copy(d):
        to = lax.rem(grp + d, NQ)
        return pltpu.make_async_remote_copy(
            src_ref=fsend.at[to], dst_ref=frecv.at[d - 1], send_sem=fs_sem.at[d - 1],
            recv_sem=fr_sem.at[d - 1], device_id={"pgrp": to}, device_id_type=MESH,
        )

    for d in range(1, NQ):
        sum_copy(d).start()
    eye = lax.broadcasted_iota(jnp.int32, (NS, NS), 0) == lax.broadcasted_iota(jnp.int32, (NS, NS), 1)
    noise = jnp.sum(jnp.where(eye, noise_ref[...], 0.0), axis=1, keepdims=True)
    total = fsend[grp]
    for d in range(1, NQ):
        sum_copy(d).wait_recv()
        total = total + frecv[d - 1]
    back = pltpu.roll(total, NP - HALF, 1)
    for n in range(NV):
        part = (total if n < 2 else back)[(n % 2) * SROWS : (n % 2) * SROWS + NS, :PART]
        out_ref[n] = part + noise * probes_ref[n].astype(F32)

    for d in range(1, NQ):
        probe_copy(d).wait_send()
        sum_copy(d).wait_send()

    def drain_share(b, _):
        n, h = lax.rem(b, NV), b // NV

        @pl.when(owner_of(h, n) != me)
        def _():
            share_copy(h, n, me).wait_send()

        return 0

    lax.fori_loop(0, NH * NV, drain_share, 0)

    @pl.when(owns)
    def _():
        def drain_params(d, _):
            param_copy(d).wait_send()
            return 0

        lax.fori_loop(1, NR, drain_params, 0)


def on_device(kernel, probes, prior_var, noise_var):
    vmem = pl.BlockSpec(memory_space=pltpu.VMEM)
    dma = pltpu.SemaphoreType.DMA
    return pl.pallas_call(
        kernel_body,
        out_shape=jax.ShapeDtypeStruct((NV, NS, PART), F32),
        in_specs=[vmem, vmem, vmem, pl.BlockSpec(memory_space=pl.ANY)],
        out_specs=vmem,
        scratch_shapes=[
            pltpu.VMEM((NS, TALL, NP), BF16),
            pltpu.VMEM((NS, ROWS, WIDE), BF16),
            pltpu.VMEM((NV, SROWS, WIDE), F32),
            pltpu.VMEM((PROWS, NP), F32),
            pltpu.VMEM((PROWS, NP), BF16),
            pltpu.VMEM((NQ - 1, PROWS, NP), BF16),
            pltpu.VMEM((NH * NV, STEP, NP), F32),
            pltpu.VMEM((NR, STEP, NP), F32),
            pltpu.VMEM((NH * NV, STEP, NP), BF16),
            pltpu.VMEM((NV, SROWS, WIDE), F32),
            pltpu.VMEM((NQ, PROWS, NP), F32),
            pltpu.VMEM((NQ - 1, PROWS, NP), F32),
            dma,
            dma((NQ - 1,)),
            dma((NQ - 1,)),
            dma((NH * NV,)),
            dma((NR,)),
            dma((NR,)),
            dma((NH * NV,)),
            dma((NQ - 1,)),
            dma((NQ - 1,)),
        ],
        compiler_params=pltpu.CompilerParams(
            collective_id=0, has_side_effects=True, vmem_limit_bytes=32 * 2**20
        ),
        cost_estimate=pl.CostEstimate(flops=2 * 10**9, bytes_accessed=2 * 10**6, transcendentals=0),
    )(probes, prior_var.reshape(1, NP), noise_var.reshape(1, NS), kernel)


def solution(mesh):
    placed = (P("srow", None, "pgrp"), P(None, "srow", "pgrp"), P("pgrp"), P("srow"))
    return jax.shard_map(
        on_device, mesh=mesh, in_specs=placed, out_specs=P(None, "srow", "pgrp"), check_vma=False
    )
```

time: 326 us -> 58.1 us (0.18)
  local copies, waits for them, and re-layouts: 220 us -> 3.91 us
  Pallas kernels: 0 us -> 53.8 us
  matrix products: 49.2 us -> 0 us
  waiting for transfers between devices: 22.2 us -> 0 us
  blocking collectives: 15.3 us -> 0 us
  starting transfers between devices: 14.6 us -> 0 us
    gather x16 -> x0, local copies, waits for them, and re-layouts: 141 us -> none  [the longest x8 70.5 us: correlate_shifted(): return lax.dynamic_slice_in_dim(padded, first + offset, length, 2)]
    transpose x9 -> x0, local copies, waits for them, and re-layouts: 66.7 us -> none  [the longest x8 66.7 us: correlate_one_turn(): window = jax.vmap(correlate_shifted, out_axes=2)(offsets)]
    pallas_call x0 -> x1, Pallas kernels: none -> 53.8 us  [on_device(): pl.pallas_call(kernel_body, out_shape=jax.ShapeDtypeStruct((NV, NS, PART)...]
    dot_general x16 -> x0, matrix products: 49.2 us -> none  [the longest x8 36.7 us: convolve_one_turn(): jnp.einsum('sjp,npjt->nst', kernel_part, window, preferred_element_type=j...]
    all_to_all x2 -> x0, waiting for transfers between devices: 22.2 us -> none  [the longest x1 12.7 us: sum_at_owner(): lax.all_to_all(in_blocks(shard, dim, length), axis, 0, 0, tiled=True)]
    all_to_all x2 -> x0, starting transfers between devices: 14.6 us -> none  [the longest x1 10.6 us: sum_at_owner(): lax.all_to_all(in_blocks(shard, dim, length), axis, 0, 0, tiled=True)]
    all_to_all x1 -> x0, blocking collectives: 8.31 us -> none  [sum_at_owner(): lax.all_to_all(in_blocks(shard, dim, length), axis, 0, 0, tiled=True)]
    dynamic_slice x9 -> x0, local copies, waits for them, and re-layouts: 8.04 us -> none  [the longest x8 7.96 us: convolve_one_turn(): kernel_part = lax.dynamic_slice_in_dim(kernel, first, width, 1)]
  transfers between devices with their start and end apart: 2 -> 0, of which waited for: 2 -> 0; matrix products, arithmetic and copies ran while one was open for 0% -> 0% of each run, Pallas kernels for 0% -> 0%
where the time goes in v1:
time: 58.1 us; the launch traced here: 57.7 us
  Pallas kernels  53.8 us (93%)
  local copies, waits for them, and re-layouts  3.91 us (7%)
    pallas_call x1, Pallas kernels, on_device(): pl.pallas_call(kernel_body, out_shape=jax.ShapeDtypeStruct((NV, NS, PART)...  53.8 us
    unnamed x7, local copies, waits for them, and re-layouts  3.28 us

profile of v1, /device:TPU:1, one launch (start us, length us, event | category | flops | bytes accessed | tf_op | source)
XLA Modules:
  0.0 57.7 jit_solution(16913136324538405942)
XLA Ops:
  0.0 0.7 %copy.5.probes_ref = bf16[4,19,56]{2,1,0:T(8,128)(2,1)S(1)} copy(bf16[4,19,56]{2,0,1:T(4,128)(2,1)} %param.5) | data formatting | bytes 17024 | tf_op args[1]
  0.7 0.0 copy-start
  0.7 1.2 %copy-done = bf16[19,224,128]{2,1,0:T(8,128)(2,1)S(1)} copy-done((bf16[19,224,128]{2,1,0:T(8,128)(2,1)S(1)}, bf16[19,224,128]{2,1,0:T(8,128)(2,1)}, u32[]{:S(2)}) %copy-start) | copy-done | bytes 1089560
  2.0 0.0 copy-start.1
  2.0 0.7 %copy-done.1 = f32[128]{0:T(128)S(1)} copy-done((f32[128]{0:T(128)S(1)}, f32[128]{0:T(128)}, u32[]{:S(2)}) %copy-start.1) | copy-done | bytes 536
  2.6 0.0 copy-start.2
  2.6 0.7 %copy-done.2 = f32[19]{0:T(128)S(1)} copy-done((f32[19]{0:T(128)S(1)}, f32[19]{0:T(128)}, u32[]{:S(2)}) %copy-start.2) | copy-done | bytes 100
  3.3 53.8 %shard_map.46 = f32[4,19,56]{2,1,0:T(8,128)S(1)} custom-call(bf16[4,19,56]{2,1,0:T(8,128)(2,1)S(1)} %copy.5.probes_ref, f32[1,128]{1,0:T(1,128)S(1)} %bitcast.2, f32[1,19]{1,0:T(1,128)S(1)} %bitcast.3, bf16[19,224,128]{2,1,0:T(8,128)(2,1)S(1)} %copy-done), custom_call_target="tpu_custom_call" | custom-call | flops 2000000000 | bytes 2000000 | tf_op jit(solution)/shard_map/pallas_call | solution.py:268
  57.1 0.6 %copy.6 = f32[4,19,56]{2,0,1:T(4,128)} copy(f32[4,19,56]{2,1,0:T(8,128)S(1)} %shard_map.46) | data formatting | bytes 34048 | tf_op jit(solution)/shard_map/pallas_call | solution.py:268
Async XLA Ops:
  0.7 1.2 %copy-start = (bf16[19,224,128]{2,1,0:T(8,128)(2,1)S(1)}, bf16[19,224,128]{2,1,0:T(8,128)(2,1)}, u32[]{:S(2)}) copy-start(bf16[19,224,128]{2,1,0:T(8,128)(2,1)} %k_hbm.1) | copy-start | bytes 3268612
  2.0 0.7 %copy-start.1 = (f32[128]{0:T(128)S(1)}, f32[128]{0:T(128)}, u32[]{:S(2)}) copy-start(f32[128]{0:T(128)} %param.6) | copy-start | bytes 1540
  2.6 0.7 %copy-start.2 = (f32[19]{0:T(128)S(1)}, f32[19]{0:T(128)}, u32[]{:S(2)}) copy-start(f32[19]{0:T(128)} %param.7) | copy-start | bytes 232

commit v2 on v1

--- a/solution.py
+++ b/solution.py
@@ -22,8 +22,9 @@
 TALL = LEAD + WIDE
 PART = NT // NQ
 HALF = 64
-SROWS = 24
-PROWS = 2 * SROWS
+SPLIT = (NS + 1) // 2
+SROWS = SPLIT * NV
+PROWS = 48
 
 
 def owner_of(h, n):
@@ -37,9 +38,9 @@
 
 
 def kernel_body(
-    probes_ref, prior_ref, noise_ref, k_hbm, out_ref,
-    kpad, base, y_ref, pf, psend, precv, rsend, rrecv, xall, f_ref, fsend, frecv,
-    k_sem, ps_sem, pr_sem, rs_sem, rr_sem, xs_sem, xr_sem, fs_sem, fr_sem,
+    probes_hbm, prior_hbm, noise_hbm, k_hbm, out_ref,
+    probes_ref, prior_ref, noise_ref, kpad, base, y_ref, pf, psend, precv, rsend, rrecv, xall, f_ref, fsend, frecv,
+    in_sem, ps_sem, pr_sem, rs_sem, rr_sem, xs_sem, xr_sem, fs_sem, fr_sem,
 ):
     me = lax.axis_index("srow")
     grp = lax.axis_index("pgrp")
@@ -61,17 +62,29 @@
         )
     lax.fori_loop(1, NR, greet, 0)
 
-    k_copy = pltpu.make_async_copy(k_hbm, kpad.at[:, pl.ds(LEAD, NT), :], k_sem)
-    k_copy.start()
-
-    pf[...] = jnp.zeros_like(pf)
-    for n in range(NV):
-        row, lane = (n % 2) * SROWS, (n // 2) * HALF
-        pf[row : row + NS, lane : lane + PART] = probes_ref[n].astype(F32)
-    psend[...] = pf[...].astype(BF16)
+    in_copies = [
+        pltpu.make_async_copy(src, dst, in_sem.at[i])
+        for i, (src, dst) in enumerate(
+            (
+                (probes_hbm, probes_ref),
+                (k_hbm, kpad.at[:, pl.ds(LEAD, NT), :]),
+                (prior_hbm, prior_ref),
+                (noise_hbm, noise_ref),
+            )
+        )
+    ]
+    for copy in in_copies:
+        copy.start()
+
     kpad[:, 0:LEAD, :] = jnp.zeros((NS, LEAD, NP), BF16)
     kpad[:, LEAD + NT : TALL, :] = jnp.zeros((NS, TALL - LEAD - NT, NP), BF16)
     f_ref[...] = jnp.zeros_like(f_ref)
+    pf[...] = jnp.zeros_like(pf)
+    in_copies[0].wait()
+    for s in range(NS):
+        row, lane = s % SPLIT * NV, s // SPLIT * HALF
+        pf[row : row + NV, lane : lane + PART] = probes_ref[s].astype(F32)
+    psend[...] = pf[...].astype(BF16)
 
     pl.semaphore_wait(barrier, NQ - 1 + NR - 1)
 
@@ -88,13 +101,13 @@
     zeros = jnp.zeros((SROWS, WIDE - NP), F32)
 
     def place(part, group):
-        for n in range(NV):
-            row, lane = (n % 2) * SROWS, (n // 2) * HALF
+        part = part[:SROWS].astype(F32)
+        for half in range(2):
+            lane = half * HALF
             inside = (lanes >= lane) & (lanes < lane + PART)
-            piece = jnp.where(inside, part[row : row + SROWS, :].astype(F32), 0.0)
-            wide = jnp.concatenate([piece, zeros], axis=1)
+            wide = jnp.concatenate([jnp.where(inside, part, 0.0), zeros], axis=1)
             shift = lax.rem(group * PART + (WIDE - (STEP - 1) - lane), WIDE)
-            y_ref[n] += pltpu.roll(wide, shift, 1)
+            y_ref[half * SROWS : (half + 1) * SROWS, :] += pltpu.roll(wide, shift, 1)
 
     y_ref[...] = jnp.zeros_like(y_ref)
     place(psend, grp)
@@ -104,16 +117,13 @@
 
     inside_wide = lax.broadcasted_iota(jnp.int32, (STEP, WIDE), 1) < NT
 
-    def make_base(s, _):
+    for s in range(NS):
         for n in range(NV):
-            line = jnp.broadcast_to(y_ref[n, pl.ds(s, 1), :], (STEP, WIDE))
+            line = jnp.broadcast_to(y_ref[s * NV + n : s * NV + n + 1, :], (STEP, WIDE))
             turned = pltpu.roll(line, 0, 1, stride=1, stride_axis=0)
             turned = jnp.where(inside_wide, turned, 0.0)
             base[s, n * STEP : (n + 1) * STEP, :] = turned.astype(BF16)
-        return 0
-
-    lax.fori_loop(0, NS, make_base, 0)
-    k_copy.wait()
+    in_copies[1].wait()
 
     def share_copy(h, n, slot):
         return pltpu.make_async_remote_copy(
@@ -127,13 +137,16 @@
     for hp in range(PAIRS):
         hs = spans(hp)
 
-        def add_sensor(s, acc):
-            w = jnp.concatenate(
-                [kpad[s, LEAD - STEP * h : LEAD - STEP * h + WIDE, :] for h in hs], axis=1
-            )
-            return acc + jnp.dot(base[s], w, preferred_element_type=F32)
-
-        acc = lax.fori_loop(0, NS, add_sensor, jnp.zeros((ROWS, NP * len(hs)), F32))
+        low = STEP * hs[0] // NP * NP
+        x = jnp.concatenate([base[s, :, low:] for s in range(NS)], axis=1)
+        w = jnp.concatenate(
+            [
+                kpad[:, LEAD - STEP * h + low : LEAD - STEP * h + WIDE, :].reshape(-1, NP)
+                for h in hs
+            ],
+            axis=1,
+        )
+        acc = jnp.dot(x, w, preferred_element_type=F32)
         for j, h in enumerate(hs):
             for n in range(NV):
                 rsend[h * NV + n] = acc[n * STEP : (n + 1) * STEP, j * NP : (j + 1) * NP]
@@ -156,6 +169,9 @@
             src_ref=xall.at[mine], dst_ref=xall.at[mine], send_sem=xs_sem.at[d],
             recv_sem=xr_sem.at[mine], device_id={"srow": to}, device_id_type=MESH,
         )
+
+    in_copies[2].wait()
+    in_copies[3].wait()
 
     @pl.when(owns)
     def _():
@@ -194,7 +210,7 @@
 
     inside_rows = lax.broadcasted_iota(jnp.int32, (ROWS, WIDE), 1) < NT
 
-    def forward_sensor(s, _):
+    for s in range(NS):
         z = jnp.zeros((ROWS, WIDE), F32)
         for hp in range(PAIRS):
             hs = spans(hp)
@@ -206,17 +222,13 @@
         z = jnp.where(inside_rows, z, 0.0)
         for n in range(NV):
             turned = pltpu.roll(z[n * STEP : (n + 1) * STEP, :], 0, 1, stride=1, stride_axis=0)
-            f_ref[n, pl.ds(s, 1), :] = jnp.sum(turned, axis=0, keepdims=True)
-        return 0
-
-    lax.fori_loop(0, NS, forward_sensor, 0)
+            f_ref[s * NV + n : s * NV + n + 1, :] = jnp.sum(turned, axis=0, keepdims=True)
 
     first = lanes < HALF
     for q in range(NQ):
-        for n in range(2):
-            low = pltpu.roll(f_ref[n], (WIDE - PART * q) % WIDE, 1)[:, :NP]
-            high = pltpu.roll(f_ref[n + 2], (WIDE - PART * q + HALF) % WIDE, 1)[:, :NP]
-            fsend[q, n * SROWS : (n + 1) * SROWS, :] = jnp.where(first, low, high)
+        low = pltpu.roll(f_ref[:SROWS], (WIDE - PART * q) % WIDE, 1)[:, :NP]
+        high = pltpu.roll(f_ref[SROWS:], (WIDE - PART * q + HALF) % WIDE, 1)[:, :NP]
+        fsend[q] = jnp.where(first, low, high)
 
     def sum_copy(d):
         to = lax.rem(grp + d, NQ)
@@ -227,16 +239,19 @@
 
     for d in range(1, NQ):
         sum_copy(d).start()
-    eye = lax.broadcasted_iota(jnp.int32, (NS, NS), 0) == lax.broadcasted_iota(jnp.int32, (NS, NS), 1)
-    noise = jnp.sum(jnp.where(eye, noise_ref[...], 0.0), axis=1, keepdims=True)
-    total = fsend[grp]
+    sensor = lax.broadcasted_iota(jnp.int32, (SROWS, NS), 0) // NV
+    column = lax.broadcasted_iota(jnp.int32, (SROWS, NS), 1)
+    line = noise_ref[...]
+    low = jnp.sum(jnp.where(column == sensor, line, 0.0), axis=1, keepdims=True)
+    high = jnp.sum(jnp.where(column == sensor + SPLIT, line, 0.0), axis=1, keepdims=True)
+    total = fsend[grp] + jnp.where(first, low, high) * pf[:SROWS]
     for d in range(1, NQ):
         sum_copy(d).wait_recv()
         total = total + frecv[d - 1]
     back = pltpu.roll(total, NP - HALF, 1)
-    for n in range(NV):
-        part = (total if n < 2 else back)[(n % 2) * SROWS : (n % 2) * SROWS + NS, :PART]
-        out_ref[n] = part + noise * probes_ref[n].astype(F32)
+    for s in range(NS):
+        row = s % SPLIT * NV
+        out_ref[s] = (total if s < SPLIT else back)[row : row + NV, :PART]
 
     for d in range(1, NQ):
         probe_copy(d).wait_send()
@@ -263,27 +278,29 @@
 
 
 def on_device(kernel, probes, prior_var, noise_var):
-    vmem = pl.BlockSpec(memory_space=pltpu.VMEM)
     dma = pltpu.SemaphoreType.DMA
-    return pl.pallas_call(
+    result = pl.pallas_call(
         kernel_body,
-        out_shape=jax.ShapeDtypeStruct((NV, NS, PART), F32),
-        in_specs=[vmem, vmem, vmem, pl.BlockSpec(memory_space=pl.ANY)],
-        out_specs=vmem,
+        out_shape=jax.ShapeDtypeStruct((NS, NV, PART), F32),
+        in_specs=[pl.BlockSpec(memory_space=pl.ANY)] * 4,
+        out_specs=pl.BlockSpec(memory_space=pltpu.VMEM),
         scratch_shapes=[
+            pltpu.VMEM((NS, NV, PART), BF16),
+            pltpu.VMEM((1, NP), F32),
+            pltpu.VMEM((1, NS), F32),
             pltpu.VMEM((NS, TALL, NP), BF16),
             pltpu.VMEM((NS, ROWS, WIDE), BF16),
-            pltpu.VMEM((NV, SROWS, WIDE), F32),
+            pltpu.VMEM((2 * SROWS, WIDE), F32),
             pltpu.VMEM((PROWS, NP), F32),
             pltpu.VMEM((PROWS, NP), BF16),
             pltpu.VMEM((NQ - 1, PROWS, NP), BF16),
             pltpu.VMEM((NH * NV, STEP, NP), F32),
             pltpu.VMEM((NR, STEP, NP), F32),
             pltpu.VMEM((NH * NV, STEP, NP), BF16),
-            pltpu.VMEM((NV, SROWS, WIDE), F32),
-            pltpu.VMEM((NQ, PROWS, NP), F32),
-            pltpu.VMEM((NQ - 1, PROWS, NP), F32),
-            dma,
+            pltpu.VMEM((2 * SROWS, WIDE), F32),
+            pltpu.VMEM((NQ, SROWS, NP), F32),
+            pltpu.VMEM((NQ - 1, SROWS, NP), F32),
+            dma((4,)),
             dma((NQ - 1,)),
             dma((NQ - 1,)),
             dma((NH * NV,)),
@@ -294,10 +311,11 @@
             dma((NQ - 1,)),
         ],
         compiler_params=pltpu.CompilerParams(
-            collective_id=0, has_side_effects=True, vmem_limit_bytes=32 * 2**20
+            collective_id=0, has_side_effects=True, vmem_limit_bytes=60 * 2**20
         ),
         cost_estimate=pl.CostEstimate(flops=2 * 10**9, bytes_accessed=2 * 10**6, transcendentals=0),
-    )(probes, prior_var.reshape(1, NP), noise_var.reshape(1, NS), kernel)
+    )(probes.transpose(1, 0, 2), prior_var.reshape(1, NP), noise_var.reshape(1, NS), kernel)
+    return result.transpose(1, 0, 2)
 
 
 def solution(mesh):

time: 58.1 us -> 39.6 us (0.68)
  Pallas kernels: 53.8 us -> 38 us
  local copies, waits for them, and re-layouts: 3.91 us -> 1.39 us
    pallas_call x1, Pallas kernels: 53.8 us -> 38 us  [on_device(): pl.pallas_call(kernel_body, out_shape=jax.ShapeDtypeStruct((NS, NV, PART)...]
    unnamed x7 -> x1, local copies, waits for them, and re-layouts: 3.28 us -> 1.39 us
    pallas_call x1 -> x0, local copies, waits for them, and re-layouts: 0.63 us -> none  [on_device(): pl.pallas_call(kernel_body, out_shape=jax.ShapeDtypeStruct((NV, NS, PART)...]
where the time goes in v2:
time: 39.6 us; the launch traced here: 39.4 us
  Pallas kernels  38 us (96%)
  local copies, waits for them, and re-layouts  1.39 us (4%)
    pallas_call x1, Pallas kernels, on_device(): pl.pallas_call(kernel_body, out_shape=jax.ShapeDtypeStruct((NS, NV, PART)...  38 us
    unnamed x1, local copies, waits for them, and re-layouts  1.39 us

profile of v2, /device:TPU:1, one launch (start us, length us, event | category | flops | bytes accessed | tf_op | source)
XLA Modules:
  0.0 39.4 jit_solution(2681226106271898937)
XLA Ops:
  0.0 38.0 %shard_map.46 = f32[19,4,56]{2,1,0:T(4,128)} custom-call(bf16[19,4,56]{2,1,0:T(4,128)(2,1)} %bitcast.5, f32[1,128]{1,0:T(1,128)} %bitcast.6, f32[1,19]{1,0:T(1,128)} %bitcast.7, bf16[19,224,128]{2,1,0:T(8,128)(2,1)} %k_hbm.1), custom_call_target="tpu_custom_call" | custom-call | flops 2000000000 | bytes 2000000 | tf_op jit(solution)/shard_map/pallas_call | solution.py:282
  38.0 1.4 %copy.6 = f32[4,19,56]{2,0,1:T(4,128)} copy(f32[4,19,56]{2,0,1:T(4,128)} %bitcast.4) | data formatting | bytes 34048

commit v3 on v2

--- a/solution.py
+++ b/solution.py
@@ -15,6 +15,7 @@
 NQ, NR = 4, 32
 STEP = 32
 NH = NT // STEP
+BLOCKS = NH * NV
 PAIRS = (NH + 1) // 2
 ROWS = NV * STEP
 WIDE = 256
@@ -27,40 +28,29 @@
 PROWS = 48
 
 
-def owner_of(h, n):
-    return 8 * n + 2 * ((n + h // 2) % 4) + h % 2
-
-
-def block_of(r):
+def owner_of(h, n, grp):
+    return 8 * n + 2 * lax.rem(n + h // 2 + grp, 4) + lax.rem(h, 2)
+
+
+def block_of(r, grp):
     n = r // 8
-    h = 2 * lax.rem(lax.rem(r // 2, 4) - n + 4, 4) + lax.rem(r, 2)
+    h = 2 * lax.rem(lax.rem(r // 2, 4) - n - grp + 8, 4) + lax.rem(r, 2)
     return h, n
 
 
 def kernel_body(
     probes_hbm, prior_hbm, noise_hbm, k_hbm, out_ref,
-    probes_ref, prior_ref, noise_ref, kpad, base, y_ref, pf, psend, precv, rsend, rrecv, xall, f_ref, fsend, frecv,
+    probes_ref, prior_ref, noise_ref, kpad, base, y_ref, pf, psend, precv, shares, rsend, rrecv, xall, f_ref,
+    fsend, frecv, t_ref,
     in_sem, ps_sem, pr_sem, rs_sem, rr_sem, xs_sem, xr_sem, fs_sem, fr_sem,
 ):
     me = lax.axis_index("srow")
     grp = lax.axis_index("pgrp")
-    my_h, my_n = block_of(me)
+    my_h, my_n = block_of(me, grp)
     mine = my_h * NV + my_n
     owns = my_h < NH
 
     barrier = pltpu.get_barrier_semaphore()
-
-    def greet(d, _):
-        pl.semaphore_signal(
-            barrier, inc=1, device_id={"srow": lax.rem(me + d, NR)}, device_id_type=MESH
-        )
-        return 0
-
-    for d in range(1, NQ):
-        pl.semaphore_signal(
-            barrier, inc=1, device_id={"pgrp": lax.rem(grp + d, NQ)}, device_id_type=MESH
-        )
-    lax.fori_loop(1, NR, greet, 0)
 
     in_copies = [
         pltpu.make_async_copy(src, dst, in_sem.at[i])
@@ -76,9 +66,18 @@
     for copy in in_copies:
         copy.start()
 
-    kpad[:, 0:LEAD, :] = jnp.zeros((NS, LEAD, NP), BF16)
-    kpad[:, LEAD + NT : TALL, :] = jnp.zeros((NS, TALL - LEAD - NT, NP), BF16)
-    f_ref[...] = jnp.zeros_like(f_ref)
+    def greet(d, _):
+        pl.semaphore_signal(
+            barrier, inc=1, device_id={"srow": lax.rem(me + d, NR)}, device_id_type=MESH
+        )
+        return 0
+
+    for d in range(1, NQ):
+        pl.semaphore_signal(
+            barrier, inc=1, device_id={"pgrp": lax.rem(grp + d, NQ)}, device_id_type=MESH
+        )
+    lax.fori_loop(1, NR, greet, 0)
+
     pf[...] = jnp.zeros_like(pf)
     in_copies[0].wait()
     for s in range(NS):
@@ -97,6 +96,9 @@
 
     for d in range(1, NQ):
         probe_copy(d).start()
+    kpad[:, 0:LEAD, :] = jnp.zeros((NS, LEAD, NP), BF16)
+    kpad[:, LEAD + NT : TALL, :] = jnp.zeros((NS, TALL - LEAD - NT, NP), BF16)
+    f_ref[...] = jnp.zeros_like(f_ref)
     lanes = lax.broadcasted_iota(jnp.int32, (SROWS, NP), 1)
     zeros = jnp.zeros((SROWS, WIDE - NP), F32)
 
@@ -127,8 +129,8 @@
 
     def share_copy(h, n, slot):
         return pltpu.make_async_remote_copy(
-            src_ref=rsend.at[h * NV + n], dst_ref=rrecv.at[slot], send_sem=rs_sem.at[h * NV + n],
-            recv_sem=rr_sem.at[slot], device_id={"srow": owner_of(h, n)}, device_id_type=MESH,
+            src_ref=rsend.at[h * NV + n], dst_ref=rrecv.at[slot], send_sem=rs_sem,
+            recv_sem=rr_sem, device_id={"srow": owner_of(h, n, grp)}, device_id_type=MESH,
         )
 
     def spans(hp):
@@ -149,15 +151,17 @@
         acc = jnp.dot(x, w, preferred_element_type=F32)
         for j, h in enumerate(hs):
             for n in range(NV):
-                rsend[h * NV + n] = acc[n * STEP : (n + 1) * STEP, j * NP : (j + 1) * NP]
+                share = acc[n * STEP : (n + 1) * STEP, j * NP : (j + 1) * NP]
+                shares[h * NV + n] = share
+                rsend[h * NV + n] = share.astype(BF16)
 
         def send_share(j, _):
             j = lax.rem(j + me, NV * len(hs))
             n, h = lax.rem(j, NV), hs[0] + j // NV
 
-            @pl.when(owner_of(h, n) != me)
+            @pl.when(owner_of(h, n, grp) != me)
             def _():
-                share_copy(h, n, me).start()
+                share_copy(h, n, lax.rem(me - owner_of(h, n, grp) + NR, NR) - 1).start()
 
             return 0
 
@@ -166,8 +170,8 @@
     def param_copy(d):
         to = lax.rem(me + d, NR)
         return pltpu.make_async_remote_copy(
-            src_ref=xall.at[mine], dst_ref=xall.at[mine], send_sem=xs_sem.at[d],
-            recv_sem=xr_sem.at[mine], device_id={"srow": to}, device_id_type=MESH,
+            src_ref=xall.at[mine], dst_ref=xall.at[mine], send_sem=xs_sem,
+            recv_sem=xr_sem, device_id={"srow": to}, device_id_type=MESH,
         )
 
     in_copies[2].wait()
@@ -175,12 +179,11 @@
 
     @pl.when(owns)
     def _():
-        def take(d, total):
-            slot = lax.rem(me + d, NR)
-            share_copy(my_h, my_n, slot).wait_recv()
-            return total + rrecv[slot]
-
-        total = lax.fori_loop(1, NR, take, rsend[mine])
+        arrived = rrecv.at[pl.ds(0, NR - 1)]
+        pltpu.make_async_copy(arrived, arrived, rr_sem).wait()
+        total = shares[mine]
+        for slot in range(NR - 1):
+            total = total + rrecv[slot].astype(F32)
         scaled = total * prior_ref[...]
         row = lax.broadcasted_iota(jnp.int32, (STEP, STEP), 0)
         col = lax.broadcasted_iota(jnp.int32, (STEP, STEP), 1)
@@ -193,17 +196,19 @@
 
         lax.fori_loop(1, NR, send_params, 0)
 
-    def wait_block(b, _):
-        @pl.when(b != mine)
-        def _():
-            pltpu.make_async_remote_copy(
-                src_ref=xall.at[b], dst_ref=xall.at[b], send_sem=xs_sem.at[0],
-                recv_sem=xr_sem.at[b], device_id={"srow": me}, device_id_type=MESH,
-            ).wait_recv()
-
-        return 0
-
-    lax.fori_loop(0, NH * NV, wait_block, 0)
+    def wait_blocks(ref, sem, count):
+        some = ref.at[pl.ds(0, count)]
+        pltpu.make_async_copy(some, some, sem).wait()
+
+    @pl.when(owns)
+    def _():
+        wait_blocks(xall, xr_sem, BLOCKS - 1)
+        wait_blocks(rsend, rs_sem, BLOCKS - 1)
+
+    @pl.when(jnp.logical_not(owns))
+    def _():
+        wait_blocks(xall, xr_sem, BLOCKS)
+        wait_blocks(rsend, rs_sem, BLOCKS)
 
     def x_of(h):
         return xall[h * NV : (h + 1) * NV].reshape(ROWS, NP)
@@ -239,6 +244,14 @@
 
     for d in range(1, NQ):
         sum_copy(d).start()
+    for d in range(1, NQ):
+        probe_copy(d).wait_send()
+
+    @pl.when(owns)
+    def _():
+        all_sent = rrecv.at[pl.ds(0, NR - 1)]
+        pltpu.make_async_copy(all_sent, all_sent, xs_sem).wait()
+
     sensor = lax.broadcasted_iota(jnp.int32, (SROWS, NS), 0) // NV
     column = lax.broadcasted_iota(jnp.int32, (SROWS, NS), 1)
     line = noise_ref[...]
@@ -248,40 +261,19 @@
     for d in range(1, NQ):
         sum_copy(d).wait_recv()
         total = total + frecv[d - 1]
-    back = pltpu.roll(total, NP - HALF, 1)
-    for s in range(NS):
-        row = s % SPLIT * NV
-        out_ref[s] = (total if s < SPLIT else back)[row : row + NV, :PART]
-
-    for d in range(1, NQ):
-        probe_copy(d).wait_send()
+    t_ref[:SROWS] = total
+    t_ref[SROWS:] = pltpu.roll(total, NP - HALF, 1)
+    for n in range(NV):
+        out_ref[n] = t_ref[pl.ds(n, NS, stride=NV), :][:, :PART]
+    for d in range(1, NQ):
         sum_copy(d).wait_send()
-
-    def drain_share(b, _):
-        n, h = lax.rem(b, NV), b // NV
-
-        @pl.when(owner_of(h, n) != me)
-        def _():
-            share_copy(h, n, me).wait_send()
-
-        return 0
-
-    lax.fori_loop(0, NH * NV, drain_share, 0)
-
-    @pl.when(owns)
-    def _():
-        def drain_params(d, _):
-            param_copy(d).wait_send()
-            return 0
-
-        lax.fori_loop(1, NR, drain_params, 0)
 
 
 def on_device(kernel, probes, prior_var, noise_var):
     dma = pltpu.SemaphoreType.DMA
-    result = pl.pallas_call(
+    return pl.pallas_call(
         kernel_body,
-        out_shape=jax.ShapeDtypeStruct((NS, NV, PART), F32),
+        out_shape=jax.ShapeDtypeStruct((NV, NS, PART), F32),
         in_specs=[pl.BlockSpec(memory_space=pl.ANY)] * 4,
         out_specs=pl.BlockSpec(memory_space=pltpu.VMEM),
         scratch_shapes=[
@@ -294,19 +286,21 @@
             pltpu.VMEM((PROWS, NP), F32),
             pltpu.VMEM((PROWS, NP), BF16),
             pltpu.VMEM((NQ - 1, PROWS, NP), BF16),
-            pltpu.VMEM((NH * NV, STEP, NP), F32),
-            pltpu.VMEM((NR, STEP, NP), F32),
-            pltpu.VMEM((NH * NV, STEP, NP), BF16),
+            pltpu.VMEM((BLOCKS, STEP, NP), F32),
+            pltpu.VMEM((BLOCKS, STEP, NP), BF16),
+            pltpu.VMEM((NR - 1, STEP, NP), BF16),
+            pltpu.VMEM((BLOCKS, STEP, NP), BF16),
             pltpu.VMEM((2 * SROWS, WIDE), F32),
             pltpu.VMEM((NQ, SROWS, NP), F32),
             pltpu.VMEM((NQ - 1, SROWS, NP), F32),
+            pltpu.VMEM((2 * SROWS, NP), F32),
             dma((4,)),
             dma((NQ - 1,)),
             dma((NQ - 1,)),
-            dma((NH * NV,)),
-            dma((NR,)),
-            dma((NR,)),
-            dma((NH * NV,)),
+            dma,
+            dma,
+            dma,
+            dma,
             dma((NQ - 1,)),
             dma((NQ - 1,)),
         ],
@@ -315,7 +309,6 @@
         ),
         cost_estimate=pl.CostEstimate(flops=2 * 10**9, bytes_accessed=2 * 10**6, transcendentals=0),
     )(probes.transpose(1, 0, 2), prior_var.reshape(1, NP), noise_var.reshape(1, NS), kernel)
-    return result.transpose(1, 0, 2)
 
 
 def solution(mesh):

time: 39.6 us -> 37.1 us (0.937)
  Pallas kernels: 38 us -> 35.5 us
    pallas_call x1, Pallas kernels: 38 us -> 35.5 us  [on_device(): pl.pallas_call(kernel_body, out_shape=jax.ShapeDtypeStruct((NV, NS, PART)...]
    pallas_call x0 -> x1, local copies, waits for them, and re-layouts: none -> 1.43 us  [on_device(): pl.pallas_call(kernel_body, out_shape=jax.ShapeDtypeStruct((NV, NS, PART)...]
    unnamed x1 -> x0, local copies, waits for them, and re-layouts: 1.39 us -> none
where the time goes in v3:
time: 37.1 us; the launch traced here: 36.9 us
  Pallas kernels  35.5 us (96%)
  local copies, waits for them, and re-layouts  1.43 us (4%)
    pallas_call x1, Pallas kernels, on_device(): pl.pallas_call(kernel_body, out_shape=jax.ShapeDtypeStruct((NV, NS, PART)...  35.5 us
    pallas_call x1, local copies, waits for them, and re-layouts, on_device(): pl.pallas_call(kernel_body, out_shape=jax.ShapeDtypeStruct((NV, NS, PART)...  1.43 us

profile of v3, /device:TPU:1, one launch (start us, length us, event | category | flops | bytes accessed | tf_op | source)
XLA Modules:
  0.0 36.9 jit_solution(1788370527843224736)
XLA Ops:
  0.0 35.5 %shard_map.46 = f32[4,19,56]{2,1,0:T(8,128)} custom-call(bf16[19,4,56]{2,1,0:T(4,128)(2,1)} %bitcast.3, f32[1,128]{1,0:T(1,128)} %bitcast.4, f32[1,19]{1,0:T(1,128)} %bitcast.5, bf16[19,224,128]{2,1,0:T(8,128)(2,1)} %k_hbm.1), custom_call_target="tpu_custom_call" | custom-call | flops 2000000000 | bytes 2000000 | tf_op jit(solution)/shard_map/pallas_call | solution.py:274
  35.5 1.4 %copy.5 = f32[4,19,56]{2,0,1:T(4,128)} copy(f32[4,19,56]{2,1,0:T(8,128)} %shard_map.46) | data formatting | bytes 34048 | tf_op jit(solution)/shard_map/pallas_call | solution.py:274

commit v4 on v3

--- a/solution.py
+++ b/solution.py
@@ -29,13 +29,23 @@
 
 
 def owner_of(h, n, grp):
-    return 8 * n + 2 * lax.rem(n + h // 2 + grp, 4) + lax.rem(h, 2)
+    return 8 * n + 2 * lax.rem(n + h // 2 + grp, 4) + h % 2
 
 
 def block_of(r, grp):
     n = r // 8
     h = 2 * lax.rem(lax.rem(r // 2, 4) - n - grp + 8, 4) + lax.rem(r, 2)
     return h, n
+
+
+def others_far_first(r):
+    x, z, y = r // 8, lax.rem(r // 2, 4), lax.rem(r, 2)
+    xs = [8 * lax.rem(x + d, 4) for d in range(4)]
+    zs = [2 * lax.rem(z + d, 4) for d in range(4)]
+    ys = [y, 1 - y]
+    steps = [(dx, dz, dy) for dx in range(4) for dz in range(4) for dy in range(2)]
+    steps.sort(key=lambda d: -(min(d[0], 4 - d[0]) + min(d[1], 4 - d[1]) + 2 * d[2]))
+    return [xs[dx] + zs[dz] + ys[dy] for dx, dz, dy in steps[:-1]]
 
 
 def kernel_body(
@@ -63,20 +73,16 @@
             )
         )
     ]
+    far_first = others_far_first(me)
+    for to in far_first:
+        pl.semaphore_signal(barrier, inc=1, device_id={"srow": to}, device_id_type=MESH)
+    for d in range(1, NQ):
+        pl.semaphore_signal(
+            barrier, inc=1, device_id={"pgrp": lax.rem(grp + d, NQ)}, device_id_type=MESH
+        )
     for copy in in_copies:
         copy.start()
 
-    def greet(d, _):
-        pl.semaphore_signal(
-            barrier, inc=1, device_id={"srow": lax.rem(me + d, NR)}, device_id_type=MESH
-        )
-        return 0
-
-    for d in range(1, NQ):
-        pl.semaphore_signal(
-            barrier, inc=1, device_id={"pgrp": lax.rem(grp + d, NQ)}, device_id_type=MESH
-        )
-    lax.fori_loop(1, NR, greet, 0)
 
     pf[...] = jnp.zeros_like(pf)
     in_copies[0].wait()
@@ -127,10 +133,11 @@
             base[s, n * STEP : (n + 1) * STEP, :] = turned.astype(BF16)
     in_copies[1].wait()
 
-    def share_copy(h, n, slot):
+    def share_copy(h, n, to):
+        slot = lax.rem(me - to + NR, NR) - 1
         return pltpu.make_async_remote_copy(
             src_ref=rsend.at[h * NV + n], dst_ref=rrecv.at[slot], send_sem=rs_sem,
-            recv_sem=rr_sem, device_id={"srow": owner_of(h, n, grp)}, device_id_type=MESH,
+            recv_sem=rr_sem, device_id={"srow": to}, device_id_type=MESH,
         )
 
     def spans(hp):
@@ -155,20 +162,16 @@
                 shares[h * NV + n] = share
                 rsend[h * NV + n] = share.astype(BF16)
 
-        def send_share(j, _):
-            j = lax.rem(j + me, NV * len(hs))
-            n, h = lax.rem(j, NV), hs[0] + j // NV
-
-            @pl.when(owner_of(h, n, grp) != me)
+        for j in range(NV * len(hs)):
+            h = hs[j // NV]
+            n = lax.rem(me // 8 + (2, 1, 3, 0)[j % NV], NV)
+            to = owner_of(h, n, grp)
+
+            @pl.when(to != me)
             def _():
-                share_copy(h, n, lax.rem(me - owner_of(h, n, grp) + NR, NR) - 1).start()
-
-            return 0
-
-        lax.fori_loop(0, NV * len(hs), send_share, 0)
-
-    def param_copy(d):
-        to = lax.rem(me + d, NR)
+                share_copy(h, n, to).start()
+
+    def param_copy(to):
         return pltpu.make_async_remote_copy(
             src_ref=xall.at[mine], dst_ref=xall.at[mine], send_sem=xs_sem,
             recv_sem=xr_sem, device_id={"srow": to}, device_id_type=MESH,
@@ -190,11 +193,8 @@
         flip = (row + col == STEP - 1).astype(BF16)
         xall[mine] = jnp.dot(flip, scaled.astype(BF16), preferred_element_type=F32).astype(BF16)
 
-        def send_params(d, _):
-            param_copy(d).start()
-            return 0
-
-        lax.fori_loop(1, NR, send_params, 0)
+        for to in far_first:
+            param_copy(to).start()
 
     def wait_blocks(ref, sem, count):
         some = ref.at[pl.ds(0, count)]
@@ -271,10 +271,11 @@
 
 def on_device(kernel, probes, prior_var, noise_var):
     dma = pltpu.SemaphoreType.DMA
+    arrays = (probes.transpose(1, 0, 2), prior_var.reshape(1, NP), noise_var.reshape(1, NS), kernel)
     return pl.pallas_call(
         kernel_body,
         out_shape=jax.ShapeDtypeStruct((NV, NS, PART), F32),
-        in_specs=[pl.BlockSpec(memory_space=pl.ANY)] * 4,
+        in_specs=[pl.BlockSpec(memory_space=pltpu.HBM)] * 4,
         out_specs=pl.BlockSpec(memory_space=pltpu.VMEM),
         scratch_shapes=[
             pltpu.VMEM((NS, NV, PART), BF16),
@@ -305,10 +306,10 @@
             dma((NQ - 1,)),
         ],
         compiler_params=pltpu.CompilerParams(
-            collective_id=0, has_side_effects=True, vmem_limit_bytes=60 * 2**20
+            collective_id=0, has_side_effects=True, vmem_limit_bytes=32 * 2**20
         ),
         cost_estimate=pl.CostEstimate(flops=2 * 10**9, bytes_accessed=2 * 10**6, transcendentals=0),
-    )(probes.transpose(1, 0, 2), prior_var.reshape(1, NP), noise_var.reshape(1, NS), kernel)
+    )(*(pltpu.with_memory_space_constraint(a, pltpu.HBM) for a in arrays))
 
 
 def solution(mesh):

time: 37.1 us -> 34.3 us (0.925)
  Pallas kernels: 35.5 us -> 33.6 us
  local copies, waits for them, and re-layouts: 1.43 us -> 0.63 us
    pallas_call x1, Pallas kernels: 35.5 us -> 33.6 us  [on_device(): pl.pallas_call(kernel_body, out_shape=jax.ShapeDtypeStruct((NV, NS, PART)...]
    pallas_call x1, local copies, waits for them, and re-layouts: 1.43 us -> 0.63 us  [on_device(): pl.pallas_call(kernel_body, out_shape=jax.ShapeDtypeStruct((NV, NS, PART)...]
where the time goes in v4:
time: 34.3 us; the launch traced here: 34.2 us
  Pallas kernels  33.6 us (98%)
  local copies, waits for them, and re-layouts  0.63 us (2%)
    pallas_call x1, Pallas kernels, on_device(): pl.pallas_call(kernel_body, out_shape=jax.ShapeDtypeStruct((NV, NS, PART)...  33.6 us

profile of v4, /device:TPU:1, one launch (start us, length us, event | category | flops | bytes accessed | tf_op | source)
XLA Modules:
  0.0 34.2 jit_solution(6794347577972414787)
XLA Ops:
  0.0 33.6 %shard_map.46 = f32[4,19,56]{2,1,0:T(8,128)S(1)} custom-call(bf16[19,4,56]{2,1,0:T(4,128)(2,1)} %bitcast.3, f32[1,128]{1,0:T(1,128)} %bitcast.4, f32[1,19]{1,0:T(1,128)} %bitcast.5, bf16[19,224,128]{2,1,0:T(8,128)(2,1)} %k_hbm.1), custom_call_target="tpu_custom_call" | custom-call | flops 2000000000 | bytes 2000000 | tf_op jit(solution)/shard_map/pallas_call | solution.py:275
  33.6 0.6 %copy.5 = f32[4,19,56]{2,0,1:T(4,128)} copy(f32[4,19,56]{2,1,0:T(8,128)S(1)} %shard_map.46) | data formatting | bytes 34048 | tf_op jit(solution)/shard_map/pallas_call | solution.py:275

commit v5 on v4

--- a/solution.py
+++ b/solution.py
@@ -44,7 +44,7 @@
     zs = [2 * lax.rem(z + d, 4) for d in range(4)]
     ys = [y, 1 - y]
     steps = [(dx, dz, dy) for dx in range(4) for dz in range(4) for dy in range(2)]
-    steps.sort(key=lambda d: -(min(d[0], 4 - d[0]) + min(d[1], 4 - d[1]) + 2 * d[2]))
+    steps.sort(key=lambda d: (-(min(d[0], 4 - d[0]) + min(d[1], 4 - d[1]) + 2 * d[2]), (d[0] * 7 + d[1] * 5 + d[2] * 3) % 11))
     return [xs[dx] + zs[dz] + ys[dy] for dx, dz, dy in steps[:-1]]
 
 
@@ -60,6 +60,11 @@
     mine = my_h * NV + my_n
     owns = my_h < NH
 
+    chip, core = grp // 2, lax.rem(grp, 2)
+
+    def mate(d):
+        return 2 * (chip if d < 2 else 1 - chip) + (core if d % 2 == 0 else 1 - core)
+
     barrier = pltpu.get_barrier_semaphore()
 
     in_copies = [
@@ -77,9 +82,7 @@
     for to in far_first:
         pl.semaphore_signal(barrier, inc=1, device_id={"srow": to}, device_id_type=MESH)
     for d in range(1, NQ):
-        pl.semaphore_signal(
-            barrier, inc=1, device_id={"pgrp": lax.rem(grp + d, NQ)}, device_id_type=MESH
-        )
+        pl.semaphore_signal(barrier, inc=1, device_id={"pgrp": mate(d)}, device_id_type=MESH)
     for copy in in_copies:
         copy.start()
 
@@ -94,13 +97,12 @@
     pl.semaphore_wait(barrier, NQ - 1 + NR - 1)
 
     def probe_copy(d):
-        to = lax.rem(grp + d, NQ)
         return pltpu.make_async_remote_copy(
             src_ref=psend, dst_ref=precv.at[d - 1], send_sem=ps_sem.at[d - 1],
-            recv_sem=pr_sem.at[d - 1], device_id={"pgrp": to}, device_id_type=MESH,
-        )
-
-    for d in range(1, NQ):
+            recv_sem=pr_sem.at[d - 1], device_id={"pgrp": mate(d)}, device_id_type=MESH,
+        )
+
+    for d in (3, 2, 1):
         probe_copy(d).start()
     kpad[:, 0:LEAD, :] = jnp.zeros((NS, LEAD, NP), BF16)
     kpad[:, LEAD + NT : TALL, :] = jnp.zeros((NS, TALL - LEAD - NT, NP), BF16)
@@ -121,7 +123,7 @@
     place(psend, grp)
     for d in range(1, NQ):
         probe_copy(d).wait_recv()
-        place(precv[d - 1], lax.rem(grp + NQ - d, NQ))
+        place(precv[d - 1], mate(d))
 
     inside_wide = lax.broadcasted_iota(jnp.int32, (STEP, WIDE), 1) < NT
 
@@ -133,10 +135,9 @@
             base[s, n * STEP : (n + 1) * STEP, :] = turned.astype(BF16)
     in_copies[1].wait()
 
-    def share_copy(h, n, to):
-        slot = lax.rem(me - to + NR, NR) - 1
+    def share_copy(block, slot, to):
         return pltpu.make_async_remote_copy(
-            src_ref=rsend.at[h * NV + n], dst_ref=rrecv.at[slot], send_sem=rs_sem,
+            src_ref=rsend.at[block], dst_ref=rrecv.at[slot], send_sem=rs_sem,
             recv_sem=rr_sem, device_id={"srow": to}, device_id_type=MESH,
         )
 
@@ -162,14 +163,12 @@
                 shares[h * NV + n] = share
                 rsend[h * NV + n] = share.astype(BF16)
 
-        for j in range(NV * len(hs)):
-            h = hs[j // NV]
-            n = lax.rem(me // 8 + (2, 1, 3, 0)[j % NV], NV)
-            to = owner_of(h, n, grp)
-
-            @pl.when(to != me)
-            def _():
-                share_copy(h, n, to).start()
+    for slot, to in enumerate(far_first):
+        h, n = block_of(to, grp)
+
+        @pl.when(h < NH)
+        def _():
+            share_copy(h * NV + n, slot, to).start()
 
     def param_copy(to):
         return pltpu.make_async_remote_copy(
@@ -179,6 +178,13 @@
 
     in_copies[2].wait()
     in_copies[3].wait()
+    first = lanes < HALF
+    sensor = lax.broadcasted_iota(jnp.int32, (SROWS, NS), 0) // NV
+    column = lax.broadcasted_iota(jnp.int32, (SROWS, NS), 1)
+    line = noise_ref[...]
+    low = jnp.sum(jnp.where(column == sensor, line, 0.0), axis=1, keepdims=True)
+    high = jnp.sum(jnp.where(column == sensor + SPLIT, line, 0.0), axis=1, keepdims=True)
+    t_ref[:SROWS] = jnp.where(first, low, high) * pf[:SROWS]
 
     @pl.when(owns)
     def _():
@@ -229,21 +235,19 @@
             turned = pltpu.roll(z[n * STEP : (n + 1) * STEP, :], 0, 1, stride=1, stride_axis=0)
             f_ref[s * NV + n : s * NV + n + 1, :] = jnp.sum(turned, axis=0, keepdims=True)
 
-    first = lanes < HALF
-    for q in range(NQ):
-        low = pltpu.roll(f_ref[:SROWS], (WIDE - PART * q) % WIDE, 1)[:, :NP]
-        high = pltpu.roll(f_ref[SROWS:], (WIDE - PART * q + HALF) % WIDE, 1)[:, :NP]
-        fsend[q] = jnp.where(first, low, high)
-
     def sum_copy(d):
-        to = lax.rem(grp + d, NQ)
         return pltpu.make_async_remote_copy(
-            src_ref=fsend.at[to], dst_ref=frecv.at[d - 1], send_sem=fs_sem.at[d - 1],
-            recv_sem=fr_sem.at[d - 1], device_id={"pgrp": to}, device_id_type=MESH,
-        )
-
-    for d in range(1, NQ):
-        sum_copy(d).start()
+            src_ref=fsend.at[d], dst_ref=frecv.at[d - 1], send_sem=fs_sem.at[d - 1],
+            recv_sem=fr_sem.at[d - 1], device_id={"pgrp": mate(d)}, device_id_type=MESH,
+        )
+
+    for d in (3, 2, 1, 0):
+        shift = WIDE - PART * mate(d)
+        low = pltpu.roll(f_ref[:SROWS], lax.rem(shift, WIDE), 1)[:, :NP]
+        high = pltpu.roll(f_ref[SROWS:], lax.rem(shift + HALF, WIDE), 1)[:, :NP]
+        fsend[d] = jnp.where(first, low, high)
+        if d > 0:
+            sum_copy(d).start()
     for d in range(1, NQ):
         probe_copy(d).wait_send()
 
@@ -252,12 +256,7 @@
         all_sent = rrecv.at[pl.ds(0, NR - 1)]
         pltpu.make_async_copy(all_sent, all_sent, xs_sem).wait()
 
-    sensor = lax.broadcasted_iota(jnp.int32, (SROWS, NS), 0) // NV
-    column = lax.broadcasted_iota(jnp.int32, (SROWS, NS), 1)
-    line = noise_ref[...]
-    low = jnp.sum(jnp.where(column == sensor, line, 0.0), axis=1, keepdims=True)
-    high = jnp.sum(jnp.where(column == sensor + SPLIT, line, 0.0), axis=1, keepdims=True)
-    total = fsend[grp] + jnp.where(first, low, high) * pf[:SROWS]
+    total = fsend[0] + t_ref[:SROWS]
     for d in range(1, NQ):
         sum_copy(d).wait_recv()
         total = total + frecv[d - 1]

time: 34.3 us -> 32.8 us (0.956)
  Pallas kernels: 33.6 us -> 32.1 us
    pallas_call x1, Pallas kernels: 33.6 us -> 32.1 us  [on_device(): pl.pallas_call(kernel_body, out_shape=jax.ShapeDtypeStruct((NV, NS, PART)...]
where the time goes in v5:
time: 32.8 us; the launch traced here: 32.7 us
  Pallas kernels  32.1 us (98%)
  local copies, waits for them, and re-layouts  0.63 us (2%)
    pallas_call x1, Pallas kernels, on_device(): pl.pallas_call(kernel_body, out_shape=jax.ShapeDtypeStruct((NV, NS, PART)...  32.1 us

profile of v5, /device:TPU:1, one launch (start us, length us, event | category | flops | bytes accessed | tf_op | source)
XLA Modules:
  0.0 32.7 jit_solution(17289977487479505949)
XLA Ops:
  0.0 32.1 %shard_map.46 = f32[4,19,56]{2,1,0:T(8,128)S(1)} custom-call(bf16[19,4,56]{2,1,0:T(4,128)(2,1)} %bitcast.3, f32[1,128]{1,0:T(1,128)} %bitcast.4, f32[1,19]{1,0:T(1,128)} %bitcast.5, bf16[19,224,128]{2,1,0:T(8,128)(2,1)} %k_hbm.1), custom_call_target="tpu_custom_call" | custom-call | flops 2000000000 | bytes 2000000 | tf_op jit(solution)/shard_map/pallas_call | solution.py:274
  32.1 0.6 %copy.5 = f32[4,19,56]{2,0,1:T(4,128)} copy(f32[4,19,56]{2,1,0:T(8,128)S(1)} %shard_map.46) | data formatting | bytes 34048 | tf_op jit(solution)/shard_map/pallas_call | solution.py:274

commit v6 on v5

--- a/solution.py
+++ b/solution.py
@@ -52,7 +52,7 @@
     probes_hbm, prior_hbm, noise_hbm, k_hbm, out_ref,
     probes_ref, prior_ref, noise_ref, kpad, base, y_ref, pf, psend, precv, shares, rsend, rrecv, xall, f_ref,
     fsend, frecv, t_ref,
-    in_sem, ps_sem, pr_sem, rs_sem, rr_sem, xs_sem, xr_sem, fs_sem, fr_sem,
+    in_sem, ps_sem, pr_sem, rs_sem, rr_sem, xs_sem, xr_sem, fs_sem, fr_sem, line_in, plane_in,
 ):
     me = lax.axis_index("srow")
     grp = lax.axis_index("pgrp")
@@ -79,8 +79,16 @@
         )
     ]
     far_first = others_far_first(me)
-    for to in far_first:
-        pl.semaphore_signal(barrier, inc=1, device_id={"srow": to}, device_id_type=MESH)
+    x, z, y = me // 8, lax.rem(me // 2, 4), lax.rem(me, 2)
+    x_line = [8 * lax.rem(x + d, 4) + 2 * z + y for d in (2, 1, 3)]
+    z_line = [8 * x + 2 * lax.rem(z + d, 4) + y for d in (2, 1, 3)]
+    y_peer = 8 * x + 2 * z + 1 - y
+
+    def greet(semaphore, to):
+        pl.semaphore_signal(semaphore, inc=1, device_id={"srow": to}, device_id_type=MESH)
+
+    for to in [y_peer, *x_line, *z_line]:
+        greet(barrier, to)
     for d in range(1, NQ):
         pl.semaphore_signal(barrier, inc=1, device_id={"pgrp": mate(d)}, device_id_type=MESH)
     for copy in in_copies:
@@ -94,7 +102,7 @@
         pf[row : row + NV, lane : lane + PART] = probes_ref[s].astype(F32)
     psend[...] = pf[...].astype(BF16)
 
-    pl.semaphore_wait(barrier, NQ - 1 + NR - 1)
+    pl.semaphore_wait(barrier, NQ - 1 + 7)
 
     def probe_copy(d):
         return pltpu.make_async_remote_copy(
@@ -104,6 +112,10 @@
 
     for d in (3, 2, 1):
         probe_copy(d).start()
+    for to in x_line:
+        greet(line_in, to)
+    pl.semaphore_wait(line_in, 3)
+    greet(plane_in, y_peer)
     kpad[:, 0:LEAD, :] = jnp.zeros((NS, LEAD, NP), BF16)
     kpad[:, LEAD + NT : TALL, :] = jnp.zeros((NS, TALL - LEAD - NT, NP), BF16)
     f_ref[...] = jnp.zeros_like(f_ref)
@@ -163,6 +175,7 @@
                 shares[h * NV + n] = share
                 rsend[h * NV + n] = share.astype(BF16)
 
+    pl.semaphore_wait(plane_in, 1)
     for slot, to in enumerate(far_first):
         h, n = block_of(to, grp)
 
@@ -303,6 +316,8 @@
             dma,
             dma((NQ - 1,)),
             dma((NQ - 1,)),
+            pltpu.SemaphoreType.REGULAR,
+            pltpu.SemaphoreType.REGULAR,
         ],
         compiler_params=pltpu.CompilerParams(
             collective_id=0, has_side_effects=True, vmem_limit_bytes=32 * 2**20

time: 32.8 us -> 30 us (0.915)
  Pallas kernels: 32.1 us -> 29.2 us
    pallas_call x1, Pallas kernels: 32.1 us -> 29.2 us  [on_device(): pl.pallas_call(kernel_body, out_shape=jax.ShapeDtypeStruct((NV, NS, PART)...]
where the time goes in v6:
time: 30 us; the launch traced here: 29.9 us
  Pallas kernels  29.2 us (97%)
  local copies, waits for them, and re-layouts  0.63 us (2%)
    pallas_call x1, Pallas kernels, on_device(): pl.pallas_call(kernel_body, out_shape=jax.ShapeDtypeStruct((NV, NS, PART)...  29.2 us
    pallas_call x1, local copies, waits for them, and re-layouts, on_device(): pl.pallas_call(kernel_body, out_shape=jax.ShapeDtypeStruct((NV, NS, PART)...  0.63 us

profile of v6, /device:TPU:1, one launch (start us, length us, event | category | flops | bytes accessed | tf_op | source)
XLA Modules:
  0.0 29.9 jit_solution(17498330321041887201)
XLA Ops:
  0.0 29.2 %shard_map.46 = f32[4,19,56]{2,1,0:T(8,128)S(1)} custom-call(bf16[19,4,56]{2,1,0:T(4,128)(2,1)} %bitcast.3, f32[1,128]{1,0:T(1,128)} %bitcast.4, f32[1,19]{1,0:T(1,128)} %bitcast.5, bf16[19,224,128]{2,1,0:T(8,128)(2,1)} %k_hbm.1), custom_call_target="tpu_custom_call" | custom-call | flops 2000000000 | bytes 2000000 | tf_op jit(solution)/shard_map/pallas_call | solution.py:287
  29.2 0.6 %copy.5 = f32[4,19,56]{2,0,1:T(4,128)} copy(f32[4,19,56]{2,1,0:T(8,128)S(1)} %shard_map.46) | data formatting | bytes 34048 | tf_op jit(solution)/shard_map/pallas_call | solution.py:287

commit v7 on v5

--- a/solution.py
+++ b/solution.py
@@ -13,6 +13,7 @@
 
 NV, NS, NT, NP = 4, 19, 224, 128
 NQ, NR = 4, 32
+ROOT = NR - 1
 STEP = 32
 NH = NT // STEP
 BLOCKS = NH * NV
@@ -52,7 +53,7 @@
     probes_hbm, prior_hbm, noise_hbm, k_hbm, out_ref,
     probes_ref, prior_ref, noise_ref, kpad, base, y_ref, pf, psend, precv, shares, rsend, rrecv, xall, f_ref,
     fsend, frecv, t_ref,
-    in_sem, ps_sem, pr_sem, rs_sem, rr_sem, xs_sem, xr_sem, fs_sem, fr_sem,
+    in_sem, ps_sem, pr_sem, rs_sem, rr_sem, xs_sem, xr_sem, fs_sem, fr_sem, all_in,
 ):
     me = lax.axis_index("srow")
     grp = lax.axis_index("pgrp")
@@ -79,10 +80,13 @@
         )
     ]
     far_first = others_far_first(me)
-    for to in far_first:
-        pl.semaphore_signal(barrier, inc=1, device_id={"srow": to}, device_id_type=MESH)
     for d in range(1, NQ):
         pl.semaphore_signal(barrier, inc=1, device_id={"pgrp": mate(d)}, device_id_type=MESH)
+
+    @pl.when(me != ROOT)
+    def _():
+        pl.semaphore_signal(barrier, inc=1, device_id={"srow": ROOT}, device_id_type=MESH)
+
     for copy in in_copies:
         copy.start()
 
@@ -94,7 +98,7 @@
         pf[row : row + NV, lane : lane + PART] = probes_ref[s].astype(F32)
     psend[...] = pf[...].astype(BF16)
 
-    pl.semaphore_wait(barrier, NQ - 1 + NR - 1)
+    pl.semaphore_wait(barrier, NQ - 1 + (NR - 1) * (me // ROOT))
 
     def probe_copy(d):
         return pltpu.make_async_remote_copy(
@@ -104,6 +108,12 @@
 
     for d in (3, 2, 1):
         probe_copy(d).start()
+
+    @pl.when(me == ROOT)
+    def _():
+        for to in far_first:
+            pl.semaphore_signal(all_in, inc=1, device_id={"srow": to}, device_id_type=MESH)
+
     kpad[:, 0:LEAD, :] = jnp.zeros((NS, LEAD, NP), BF16)
     kpad[:, LEAD + NT : TALL, :] = jnp.zeros((NS, TALL - LEAD - NT, NP), BF16)
     f_ref[...] = jnp.zeros_like(f_ref)
@@ -162,6 +172,10 @@
                 share = acc[n * STEP : (n + 1) * STEP, j * NP : (j + 1) * NP]
                 shares[h * NV + n] = share
                 rsend[h * NV + n] = share.astype(BF16)
+
+    @pl.when(me != ROOT)
+    def _():
+        pl.semaphore_wait(all_in, 1)
 
     for slot, to in enumerate(far_first):
         h, n = block_of(to, grp)
@@ -221,19 +235,37 @@
 
     inside_rows = lax.broadcasted_iota(jnp.int32, (ROWS, WIDE), 1) < NT
 
-    for s in range(NS):
-        z = jnp.zeros((ROWS, WIDE), F32)
-        for hp in range(PAIRS):
-            hs = spans(hp)
-            x = jnp.concatenate([x_of(h) for h in hs], axis=1)
-            w = jnp.concatenate(
-                [kpad[s, LEAD - STEP * h : LEAD - STEP * h + WIDE, :] for h in hs], axis=1
-            )
-            z = z + lax.dot_general(x, w, (((1,), (1,)), ((), ())), preferred_element_type=F32)
-        z = jnp.where(inside_rows, z, 0.0)
-        for n in range(NV):
-            turned = pltpu.roll(z[n * STEP : (n + 1) * STEP, :], 0, 1, stride=1, stride_axis=0)
-            f_ref[s * NV + n : s * NV + n + 1, :] = jnp.sum(turned, axis=0, keepdims=True)
+    upper = lax.broadcasted_iota(jnp.int32, (ROWS, NP), 1) < NT - NP
+    x_all = jnp.concatenate([x_of(h) for h in range(NH)], axis=1)
+    few = NP // STEP
+
+    def halves_of(sensors, at, count):
+        w = jnp.concatenate(
+            [
+                jnp.concatenate(
+                    [kpad[s, LEAD - STEP * h + at : LEAD - STEP * h + at + NP, :] for h in range(count)],
+                    axis=1,
+                )
+                for s in sensors
+            ],
+            axis=0,
+        )
+        return lax.dot_general(
+            x_all[:, : count * NP], w, (((1,), (1,)), ((), ())), preferred_element_type=F32
+        )
+
+    def forward_sensors(sensors):
+        low = halves_of(sensors, 0, few)
+        high = halves_of(sensors, NP, NH)
+        for i, s in enumerate(sensors):
+            lane = slice(i * NP, (i + 1) * NP)
+            z = jnp.concatenate([low[:, lane], jnp.where(upper, high[:, lane], 0.0)], axis=1)
+            for n in range(NV):
+                turned = pltpu.roll(z[n * STEP : (n + 1) * STEP, :], 0, 1, stride=1, stride_axis=0)
+                f_ref[s * NV + n : s * NV + n + 1, :] = jnp.sum(turned, axis=0, keepdims=True)
+
+    for s in range(0, NS, 2):
+        forward_sensors(range(s, min(s + 2, NS)))
 
     def sum_copy(d):
         return pltpu.make_async_remote_copy(
@@ -303,6 +335,7 @@
             dma,
             dma((NQ - 1,)),
             dma((NQ - 1,)),
+            pltpu.SemaphoreType.REGULAR,
         ],
         compiler_params=pltpu.CompilerParams(
             collective_id=0, has_side_effects=True, vmem_limit_bytes=32 * 2**20

time: 32.8 us -> 29.5 us (0.90)
  Pallas kernels: 32.1 us -> 28.8 us
    pallas_call x1, Pallas kernels: 32.1 us -> 28.8 us  [on_device(): pl.pallas_call(kernel_body, out_shape=jax.ShapeDtypeStruct((NV, NS, PART)...]
where the time goes in v7:
time: 29.5 us; the launch traced here: 29.4 us
  Pallas kernels  28.8 us (98%)
  local copies, waits for them, and re-layouts  0.63 us (2%)
    pallas_call x1, Pallas kernels, on_device(): pl.pallas_call(kernel_body, out_shape=jax.ShapeDtypeStruct((NV, NS, PART)...  28.8 us
    pallas_call x1, local copies, waits for them, and re-layouts, on_device(): pl.pallas_call(kernel_body, out_shape=jax.ShapeDtypeStruct((NV, NS, PART)...  0.63 us

profile of v7, /device:TPU:1, one launch (start us, length us, event | category | flops | bytes accessed | tf_op | source)
XLA Modules:
  0.0 29.4 jit_solution(1017972893820772677)
XLA Ops:
  0.0 28.8 %shard_map.46 = f32[4,19,56]{2,1,0:T(8,128)S(1)} custom-call(bf16[19,4,56]{2,1,0:T(4,128)(2,1)} %bitcast.3, f32[1,128]{1,0:T(1,128)} %bitcast.4, f32[1,19]{1,0:T(1,128)} %bitcast.5, bf16[19,224,128]{2,1,0:T(8,128)(2,1)} %k_hbm.1), custom_call_target="tpu_custom_call" | custom-call | flops 2000000000 | bytes 2000000 | tf_op jit(solution)/shard_map/pallas_call | solution.py:306
  28.8 0.6 %copy.5 = f32[4,19,56]{2,0,1:T(4,128)} copy(f32[4,19,56]{2,1,0:T(8,128)S(1)} %shard_map.46) | data formatting | bytes 34048 | tf_op jit(solution)/shard_map/pallas_call | solution.py:306
